TPU v7x, 32 devices: a whole 2x2x4 slice. The times are simulated.
32 devices in a mesh: row: 4 (over y, x), col: 8 (over z, core).
Axes of the slice: x: 2, y: 2, z: 4, core: 2. Of those that a mesh axis runs over, the one named last changes fastest.
Arguments:
- amplitudes: bfloat16 [6144, 4096], P('row', 'col'), may hold values from -6 to 6
- integrals: bfloat16 [4096, 4096], P('row', 'col'), may hold values from -0.125 to 0.125
- screen_mask: int32 [48, 32], P('row', 'col'), may hold values from 0 to 1, as said below
- tile_order: int32 [32], replicated, may hold values from 0 to 31, each once
Outputs:
- ladder: float32 [6144, 4096], P('row', 'col')
Inputs may be any that keep to these rules, and one draw needn't show every extreme that they name: `screen_mask`: in every aligned block of 12 tile rows by 4 tile columns exactly 24 tiles survive; rows of tiles hold different numbers of them. `tile_order`: each number of 0 to 31 appears once.
All inputs are finite; a program needn't handle non-finite values.
Results may differ from a plain program's by a relative error of at most 0.0003.
Values may be sent and summed in bfloat16 or wider, within the bound.
No kernel may reach another device: no remote copies, remote signals or barrier semaphores. Data moves between devices by JAX's collectives and lax.ppermute only.
A program may use at most 256 MiB of HBM per device.

v0:
```python
import jax
import jax.numpy as jnp
from jax import lax
from jax.sharding import PartitionSpec as P

TILE_PAIRS = 128


def accumulate(left, right):
    return jnp.dot(left, right, preferred_element_type=jnp.float32)


def ordered_rows(integrals, tile_order):
    result_cols = integrals.shape[1]
    all_tiles = tile_order.shape[0]
    gathered = lax.all_gather(integrals, "row", axis=0, tiled=True)
    return jnp.take(
        gathered.reshape(all_tiles, TILE_PAIRS, result_cols), tile_order, axis=0
    ).reshape(all_tiles * TILE_PAIRS, result_cols)


def local(amplitudes, integrals, screen_mask, tile_order):
    local_rows = amplitudes.shape[0]
    local_cols = amplitudes.shape[1]
    row_tiles = local_rows // TILE_PAIRS
    col_tiles = local_cols // TILE_PAIRS
    weight_values = screen_mask.astype(jnp.bfloat16)[:, None, :, None]
    screened_tiles = (
        amplitudes.reshape(row_tiles, TILE_PAIRS, col_tiles, TILE_PAIRS) * weight_values
    ).reshape(local_rows, local_cols)
    ordered = ordered_rows(integrals, tile_order)
    return accumulate(lax.all_gather(screened_tiles, "col", axis=1, tiled=True), ordered)


def solution(mesh):
    placed = (P("row", "col"), P("row", "col"), P("row", "col"), P())
    return jax.shard_map(
        local, mesh=mesh, in_specs=placed, out_specs=P("row", "col"), check_vma=False
    )
```

profile of v0, /device:TPU:0, one launch (start us, length us, event | category | flops | bytes accessed | tf_op | source)
XLA Modules:
  0.0 201.8 jit_solution(2962326857522092449)
XLA Ops:
  6.5 0.0 all-gather.5.cloned.1.call-start
  6.5 0.7 all-gather.5.cloned.1.call-update
  7.3 0.0 copy-start
  7.3 0.0 all-gather.3.cloned.1.call-start
  7.3 0.7 convert_element_type.3
  8.0 0.1 copy.5
  8.1 0.5 mul.11
  8.6 2.8 %bitcast_multiply_fusion = bf16[1536,512]{1,0:T(8,128)(2,1)} fusion(bf16[1536,512]{1,0:T(8,128)(2,1)} %param.4, bf16[192,8,4,128]{3,2,1,0:T(4,128)(2,1)S(1)} %bitcast.11), kind=kLoop, calls=%fused_computation.2 | loop fusion | flops 786432 | bytes 4718592 | tf_op jit(solution)/shard_map/mul | solution.py:29
  11.4 0.0 all-gather.3.cloned.1.call-update
  11.4 0.0 copy-done
  11.4 0.1 broadcast_bitcast_fusion
  11.5 53.1 %all-gather.5.cloned.1.call-done = bf16[4096,512]{1,0:T(8,128)(2,1)} async-done(((bf16[1024,512]{1,0:T(8,128)(2,1)}), bf16[4096,512]{1,0:T(8,128)(2,1)}) %all-gather.5.cloned.1.call-update) | async-done | bytes 4194320 | tf_op jit(solution)/shard_map/all_gather | solution.py:16
  64.6 4.9 %gather_fusion = bf16[32,128,512]{2,1,0:T(8,128)(2,1)} fusion(bf16[32,128,512]{2,1,0:T(8,128)(2,1)} %bitcast.12, s32[1024]{0:T(1024)S(1)} %pad_clamp_fusion), kind=kCustom, calls=%fused_computation | custom fusion | bytes 8388736 | tf_op jit(solution)/shard_map/jit(_take)/gather | solution.py:17
  69.6 3.9 %bitcast_select_fusion = bf16[4096,512]{1,0:T(8,128)(2,1)} fusion(bf16[32,128,512]{2,1,0:T(8,128)(2,1)} %gather_fusion, pred[4096]{0:T(1024)(128)(4,1)S(1)} %broadcast_bitcast_fusion), kind=kLoop, calls=%fused_computation.1 | loop fusion | flops 2097152 | bytes 8392704 | tf_op jit(solution)/shard_map/jit(_take)/select_n | solution.py:17
  73.5 109.5 %all-gather.3.cloned.1.call-done = bf16[1536,4096]{1,0:T(8,128)(2,1)} async-done(((bf16[1536,512]{1,0:T(8,128)(2,1)}), bf16[1536,4096]{1,0:T(8,128)(2,1)}) %all-gather.3.cloned.1.call-update) | async-done | bytes 12582928 | tf_op jit(solution)/shard_map/all_gather | solution.py:32
  183.0 12.0 %fusion = f32[1536,512]{1,0:T(8,128)} fusion(bf16[1536,4096]{1,0:T(8,128)(2,1)} %all-gather.3.cloned.1.call-done, bf16[4096,512]{1,0:T(8,128)(2,1)} %bitcast_select_fusion), kind=kOutput, calls=%fused_computation.7 | convolution fusion | flops 6442450944 | bytes 19922944 | tf_op jit(solution)/shard_map/dot_general | solution.py:10
  (3 shorter events, 0.0 us)
Async XLA Ops:
  6.5 58.1 %all-gather.5.cloned.1.call-start = ((), (), s32[]{:S(2)}) async-start(), calls=%async_computation.1 | async-start | bytes 5242880 | tf_op jit(solution)/shard_map/all_gather | solution.py:16
  7.3 4.1 %copy-start = (s32[32]{0:T(128)S(1)}, s32[32]{0:T(128)}, u32[]{:S(2)}) copy-start(s32[32]{0:T(128)} %param.7) | copy-start | bytes 388
  7.3 175.7 %all-gather.3.cloned.1.call-start = ((), (), s32[]{:S(2)}) async-start(), calls=%async_computation | async-start | bytes 14155776 | tf_op jit(solution)/shard_map/all_gather | solution.py:32
Sparse Core Ops, SparseCore 0:
  9.2 55.3 all-gather.4
  66.2 116.7 all-gather.2
where the time goes:
time: 202 us
  waiting for transfers between devices  163 us (81%)
  between operations  13.4 us (7%)
  matrix products  12 us (6%)
  other arithmetic  7.41 us (4%)
  local copies, waits for them, and re-layouts  5.6 us (3%)
    all_gather x1, waiting for transfers between devices, local(): lax.all_gather(screened_tiles, 'col', axis=1, tiled=True)  109 us
    all_gather x1, waiting for transfers between devices, ordered_rows(): gathered = lax.all_gather(integrals, 'row', axis=0, tiled=True)  53.1 us
    dot_general x1, matrix products, accumulate(): return jnp.dot(left, right, preferred_element_type=jnp.float32)  12 us
    gather x1, local copies, waits for them, and re-layouts, ordered_rows(): jnp.take(gathered.reshape(all_tiles, TILE_PAIRS, result_cols), tile_order...  4.94 us
  transfers between devices with their start and end apart: 2, of which 2 were waited for; matrix products, arithmetic and copies ran while one was open for 6% of the time, Pallas kernels for 0%

commit v1 on v0

v1 whole, which is shorter than its diff:
```python
import functools

import jax
import jax.numpy as jnp
from jax import lax
from jax.experimental import pallas as pl
from jax.experimental.pallas import tpu as pltpu
from jax.sharding import PartitionSpec as P

TILE = 128
CAP = 24
META = 16
ROWS = 512
LANES = 128
SWAP = CAP * TILE + META
BLOCK = SWAP + META
SMEM = pl.BlockSpec(memory_space=pltpu.SMEM)
VMEM = pl.BlockSpec(memory_space=pltpu.VMEM)
ANY = pl.BlockSpec(memory_space=pl.ANY)


ORDER = {
    ("line", 2, 0): [("swap", 0, 0)],
    ("line", 2, 1): [("swap", 1, 0), ("side", 1, 0), ("side", 2, 0)],
    ("swap", 2, 1): [("side", 3, 0)],
    ("swap", 1, 1): [("line", 2, 0)],
}


def nbytes(shape, dtype):
    size = jnp.dtype(dtype).itemsize
    for extent in shape:
        size *= extent
    return size


def with_vmem(arrays):
    need = sum(nbytes(shape, dtype) for shape, dtype in arrays)
    return pltpu.CompilerParams(vmem_limit_bytes=need + 6 * 1024 * 1024)


def in_hbm(x):
    return pltpu.with_memory_space_constraint(x, pltpu.HBM)


def in_vmem(x):
    return pltpu.with_memory_space_constraint(x, pltpu.VMEM)


def dot(left, right):
    return jnp.dot(left, right, preferred_element_type=jnp.float32)


def pack_kernel(mask_hbm, amplitudes_ref, packed, mask_ref, amplitudes, mask_sem, in_sems):
    col_tiles, row_tiles = mask_ref.shape
    mask_copy = pltpu.make_async_copy(mask_hbm, mask_ref, mask_sem)
    mask_copy.start()
    copies = []
    for i in range(row_tiles):
        at = pl.ds(i * TILE, TILE)
        copies.append(
            pltpu.make_async_copy(amplitudes_ref.at[at], amplitudes.at[at], in_sems.at[i])
        )
        copies[i].start()
    lane = lax.broadcasted_iota(jnp.int32, (META, LANES), 1)
    places = jnp.full((META, LANES), CAP, jnp.int32)
    slot = jnp.int32(0)
    mask_copy.wait()
    for i in range(row_tiles):
        copies[i].wait()
        for k in range(col_tiles):
            keep = mask_ref[k, i] != 0

            @pl.when(keep)
            def _(i=i, k=k, slot=slot):
                to = pl.ds(pl.multiple_of(slot * TILE, TILE), TILE)
                packed[to] = amplitudes[pl.ds(i * TILE, TILE), pl.ds(k * TILE, TILE)]

            places = jnp.where(lane == i * col_tiles + k, jnp.where(keep, slot, CAP), places)
            slot = slot + keep.astype(jnp.int32)
    packed[pl.ds(CAP * TILE, META)] = places.astype(jnp.float32).astype(packed.dtype)


def pack(mask, amplitudes):
    shape = (BLOCK, TILE)
    dtype = amplitudes.dtype
    return pl.pallas_call(
        pack_kernel,
        out_shape=pltpu.VMEM(shape, dtype),
        in_specs=[ANY, ANY],
        out_specs=VMEM,
        scratch_shapes=[
            pltpu.SMEM(mask.shape[::-1], mask.dtype),
            pltpu.VMEM(amplitudes.shape, dtype),
            pltpu.SemaphoreType.DMA,
            pltpu.SemaphoreType.DMA((mask.shape[0],)),
        ],
        compiler_params=with_vmem([(amplitudes.shape, dtype)]),
        cost_estimate=pl.CostEstimate(
            flops=0, bytes_accessed=3 * nbytes(shape, dtype), transcendentals=0
        ),
        name="pack",
    )(in_hbm(mask.T), in_hbm(amplitudes))


def unpacked(places_ref, table, rows, packed, col_tiles):
    lines = []
    for i in range(ROWS // TILE):
        line = []
        for k in range(col_tiles):
            place = places_ref[table, 0, (rows * (ROWS // TILE) + i) * col_tiles + k]
            at = pl.multiple_of(jnp.minimum(place, CAP - 1) * TILE, TILE)
            tile = packed[pl.ds(at, TILE)]
            line.append(jnp.where(place < CAP, tile, jnp.zeros_like(tile)))
        lines.append(jnp.concatenate(line, axis=1))
    return jnp.concatenate(lines, axis=0)


def places_of(packed):
    return packed[pl.ds(CAP * TILE, META)].astype(jnp.float32).astype(jnp.int32)[:8]


def near_kernel(chips, row_devices, steps, b_count, order_ref, *refs):
    refs = list(refs)
    pieces = [(refs.pop(0), refs.pop(0)) for _ in steps]
    b_refs = [refs.pop(0) for _ in range(b_count)]
    total, far_rows, b_all, ordered, places_vmem, places, places_sem = refs

    row = lax.axis_index("row")
    col = lax.axis_index("col")
    chip, core = col // 2, col % 2
    b_tiles = b_all.shape[0] // row_devices // TILE
    col_tiles = ordered.shape[0] // TILE // 2

    for e, piece in enumerate(pieces):
        for side, ref in enumerate(piece):
            places_vmem[2 * e + side] = places_of(ref)
    places_copy = pltpu.make_async_copy(places_vmem, places, places_sem)
    places_copy.start()
    total[...] = jnp.zeros_like(total)
    start = 0
    for ref in b_refs:
        size = ref.shape[0]
        b_all[pl.ds(start, size)] = ref[...]
        start += size

    def order_rows(from_chip, first_core, into):
        for side in range(2):
            for k in range(col_tiles):
                place = first_core if side == 0 else 1 - first_core
                tile = order_ref[(from_chip * 2 + place) * col_tiles + k]
                at = ((tile // b_tiles) ^ row) * b_tiles + tile % b_tiles
                into[pl.ds((side * col_tiles + k) * TILE, TILE)] = b_all[
                    pl.ds(pl.multiple_of(at * TILE, TILE), TILE)
                ]

    order_rows(jnp.where(chip == 0, chips - 1, 0), 0, far_rows)
    places_copy.wait()

    for e, step in enumerate(steps):
        source = chip + (2 * core - 1) * step

        @pl.when((source >= 0) & (source < chips))
        def _(e=e, step=step, source=source):
            order_rows(source, core if step >= 0 else 1 - core, ordered)

            @pl.loop(0, total.shape[0] // ROWS)
            def _(m):
                at = pl.ds(pl.multiple_of(m * ROWS, ROWS), ROWS)
                left = [
                    unpacked(places, 2 * e + side, m, pieces[e][side], col_tiles)
                    for side in range(2)
                ]
                total[at] += dot(jnp.concatenate(left, axis=1), ordered[...])


def near(chips, row_devices, steps, order, pieces, b_parts, shape, col_tiles):
    local_rows, result_cols = shape
    dtype = b_parts[0].dtype
    depth = 2 * col_tiles * TILE
    flat = [chunk for piece in pieces for chunk in piece] + b_parts
    blocks = 2 * len(steps)
    b_rows = sum(part.shape[0] for part in b_parts)
    scratch = [
        ((b_rows, result_cols), dtype),
        ((depth, result_cols), dtype),
        ((blocks, 8, LANES), jnp.int32),
    ]
    outs = [(shape, jnp.float32), ((depth, result_cols), dtype)]
    return pl.pallas_call(
        functools.partial(near_kernel, chips, row_devices, steps, len(b_parts)),
        out_shape=[pltpu.VMEM(*entry) for entry in outs],
        in_specs=[SMEM] + [VMEM] * len(flat),
        out_specs=[VMEM] * 2,
        scratch_shapes=[pltpu.VMEM(*entry) for entry in scratch] + [
            pltpu.SMEM((blocks, 8, LANES), jnp.int32),
            pltpu.SemaphoreType.DMA,
        ],
        compiler_params=with_vmem(scratch),
        cost_estimate=pl.CostEstimate(flops=0, bytes_accessed=0, transcendentals=0),
        name="near",
    )(in_hbm(order), *[in_vmem(x) for x in flat])


def far_kernel(chips, block, last, mine, other, far_rows, total_in, total_out, *refs):
    refs = list(refs)
    total = refs.pop(0) if last else total_out
    places_vmem, places, places_sem = refs[:3]
    col = lax.axis_index("col")
    chip, core = col // 2, col % 2
    depth = far_rows.shape[0] // 2
    outs = [None] * (total.shape[0] // ROWS)
    if last:
        for m in range(len(outs)):
            at = pl.ds(m * ROWS, ROWS)
            outs[m] = pltpu.make_async_copy(total.at[at], total_out.at[at], refs[3].at[m])

    for ref, stream in ((mine, core), (other, 1 - core)):

        @pl.when(chip == (chips - 1) * (1 - stream))
        def _(ref=ref, stream=stream):
            places_vmem[...] = places_of(ref)
            copy = pltpu.make_async_copy(places_vmem, places.at[0], places_sem)
            copy.start()
            start = pl.multiple_of((stream ^ block) * depth, depth)
            right = far_rows[pl.ds(start, depth)]
            copy.wait()
            for m, out in enumerate(outs):
                at = pl.ds(m * ROWS, ROWS)
                total[at] = total_in[at] + dot(unpacked(places, 0, m, ref, depth // TILE), right)
                if last:
                    out.start()

    if last:

        @pl.when((chip != 0) & (chip != chips - 1))
        def _():
            for m, out in enumerate(outs):
                at = pl.ds(m * ROWS, ROWS)
                total[at] = total_in[at]
                out.start()

        for out in outs:
            out.wait()


def far(chips, block, mine, other, far_rows, total, last):
    shape = total.shape
    local_rows, result_cols = shape
    scratch = [((8, LANES), jnp.int32)]
    if last:
        scratch.insert(0, (shape, jnp.float32))
    sems = [pltpu.SemaphoreType.DMA((local_rows // ROWS,))] if last else []
    return pl.pallas_call(
        functools.partial(far_kernel, chips, block, last),
        out_shape=(pltpu.HBM if last else pltpu.VMEM)(shape, jnp.float32),
        in_specs=[VMEM] * 4,
        out_specs=ANY if last else VMEM,
        input_output_aliases={} if last else {3: 0},
        scratch_shapes=[pltpu.VMEM(*entry) for entry in scratch] + [
            pltpu.SMEM((1, 8, LANES), jnp.int32),
            pltpu.SemaphoreType.DMA,
        ] + sems,
        compiler_params=with_vmem(scratch),
        cost_estimate=pl.CostEstimate(
            flops=local_rows * result_cols * far_rows.shape[0], bytes_accessed=8 * 1024 * 1024,
            transcendentals=0,
        ),
        name="far",
    )(*[in_vmem(x) for x in (mine, other, far_rows, total)])


def after(chunk, others):
    return lax.optimization_barrier((chunk, *others))[0] if others else chunk


class Transfers:
    def __init__(self, row_devices, chips, own, integrals):
        self.row_devices = row_devices
        self.chips = chips
        self.integrals = integrals
        self.made = {("own", 0, 0): own, ("side", 0, 0): integrals}

    def get(self, name):
        if name not in self.made:
            self.made[name] = getattr(self, name[0])(name, *name[1:])
        return self.made[name]

    def held(self, name):
        return name[1] < (self.row_devices if name[0] == "side" else self.chips)

    def send(self, chunk, axis, perm, name):
        others = [self.get(other) for other in ORDER.get(name, ()) if self.held(other)]
        return lax.ppermute(after(chunk, others), axis, perm)

    def line(self, name, step, i):
        cross = i if step == 1 else 0
        below, above = range(step, self.chips), range(self.chips - step)
        perm = [(2 * (z - 1) + cross, 2 * z) for z in below]
        perm += [(2 * (z + 1) + 1 - cross, 2 * z + 1) for z in above]
        chunk = self.get(("own", 0, 0) if step == 1 else ("line", step - 1, i))
        return self.send(chunk, "col", perm, name)

    def swap(self, name, step, i):
        perm = [(2 * z, 2 * z + 1) for z in range(step, self.chips)]
        perm += [(2 * z + 1, 2 * z) for z in range(self.chips - step)]
        chunk = self.get(("line", step, i) if step else ("own", 0, 0))[:SWAP]
        return self.send(chunk, "col", perm, name)

    def half(self, d, h):
        if d & (d - 1):
            return self.get(("side", d, h))
        rows = self.integrals.shape[0] // 2
        return self.get(("side", d, 0))[h * rows : (h + 1) * rows]

    def side(self, name, d, h):
        if d & (d - 1):
            bit = d & -d if h else 1 << (d.bit_length() - 1)
            chunk = self.half(d ^ bit, h)
        else:
            bit, chunk = d, self.integrals
        perm = [(r, r ^ bit) for r in range(self.row_devices)]
        return self.send(chunk, "row", perm, name)


def local(row_devices, col_devices, amplitudes, integrals, screen_mask, tile_order):
    chips = col_devices // 2
    own = pack(screen_mask, amplitudes)
    moves = Transfers(row_devices, chips, own, integrals)
    sides = [("side", d, h) for d in range(row_devices) for h in range(2 if d & (d - 1) else 1)]
    steps = [0]
    pieces = [(own, moves.get(("swap", 0, 0)))]
    for step in range(1, chips - 1):
        for kind in ("line", "swap"):
            steps.append(step if kind == "line" else -step)
            pieces.append([moves.get((kind, step, i)) for i in range(2)])
    total, far_rows = near(
        chips, row_devices, steps, tile_order, pieces, [moves.get(side) for side in sides],
        (amplitudes.shape[0], integrals.shape[1]), screen_mask.shape[1],
    )
    last = []
    for i in range(2):
        name = ("line", chips - 1, i)
        moves.made[name], total = lax.optimization_barrier((moves.get(name), total))
        last.append((moves.made[name], moves.get(("swap", chips - 1, i))))
    for i, (block, other) in enumerate(last):
        total = far(chips, i, block, other, far_rows, total, i == len(last) - 1)
    return total


def solution(mesh):
    placed = (P("row", "col"), P("row", "col"), P("row", "col"), P())
    return jax.shard_map(
        functools.partial(local, mesh.shape["row"], mesh.shape["col"]),
        mesh=mesh, in_specs=placed, out_specs=P("row", "col"), check_vma=False,
    )
```

time: 202 us -> 70 us (0.35)
  the two profiles are of different devices: /device:TPU:0 before, /device:TPU:31 now
where the time goes in v1:
time: 70 us; the launch traced here: 69.7 us
  waiting for transfers between devices  36.8 us (53%)
  starting transfers between devices  17.3 us (25%)
  Pallas kernels  14.9 us (21%)
    ppermute x17, waiting for transfers between devices, send(): return lax.ppermute(after(chunk, others), axis, perm)  36.8 us
    ppermute x17, starting transfers between devices, send(): return lax.ppermute(after(chunk, others), axis, perm)  17.3 us
    pallas_call x1, Pallas kernels, near(): pl.pallas_call(functools.partial(near_kernel, chips, row_devices, steps,...  8.8 us
    pallas_call x2, Pallas kernels, far(): pl.pallas_call(functools.partial(far_kernel, chips, block, last), out_sha...  4.43 us
    pallas_call x1, Pallas kernels, pack(): pl.pallas_call(pack_kernel, out_shape=pltpu.VMEM(shape, dtype), in_specs=...  1.61 us
  transfers between devices with their start and end apart: 17, of which 7 were waited for; matrix products, arithmetic and copies ran while one was open for 1% of the time, Pallas kernels for 15%

profile of v1, /device:TPU:31, one launch (start us, length us, event | category | flops | bytes accessed | tf_op | source)
XLA Modules:
  0.0 69.7 jit_solution(16594702011081354622)
XLA Ops:
  0.0 1.6 %pack.1.refs_0_ = bf16[3104,128]{1,0:T(8,128)(2,1)S(1)} custom-call(s32[4,12]{1,0:T(4,128)} %bitcast.1, bf16[1536,512]{1,0:T(8,128)(2,1)} %amplitudes_ref.1), custom_call_target="tpu_custom_call" | custom-call | bytes 2383872 | tf_op jit(solution)/shard_map/pack/pallas_call | solution.py:87
  1.6 2.1 %collective-permute-start.1 = (bf16[3104,128]{1,0:T(8,128)(2,1)S(1)}, bf16[3104,128]{1,0:T(8,128)(2,1)S(1)}, u32[]{:S(2)}, u32[]{:S(2)}) collective-permute-start(bf16[3104,128]{1,0:T(8,128)(2,1)S(1)} %pack.1.refs_0_), channel_id=1, source_target_pairs={{0,2},{2,4},{4,6},{3,1},{5,3},{7,5},{8,10},{10,12},{12,14},{11,9},... | collective-permute-start | bytes 2383880 | tf_op jit(solution)/shard_map/ppermute | solution.py:294
  3.8 0.3 collective-permute-start.3
  4.1 0.2 collective-permute-start.4
  4.3 0.7 %collective-permute-start = (bf16[3104,128]{1,0:T(8,128)(2,1)S(1)}, bf16[3104,128]{1,0:T(8,128)(2,1)S(1)}, u32[]{:S(2)}, u32[]{:S(2)}) collective-permute-start(bf16[3104,128]{1,0:T(8,128)(2,1)S(1)} %pack.1.refs_0_), channel_id=1, source_target_pairs={{1,2},{3,4},{5,6},{2,1},{4,3},{6,5},{9,10},{11,12},{13,14},{10,9},... | collective-permute-start | bytes 2383880 | tf_op jit(solution)/shard_map/ppermute | solution.py:294
  5.0 0.1 slice.37
  5.1 1.8 %collective-permute-start.7 = (bf16[3088,128]{1,0:T(8,128)(2,1)S(1)}, bf16[3088,128]{1,0:T(8,128)(2,1)S(1)}, u32[]{:S(2)}, u32[]{:S(2)}) collective-permute-start(bf16[3088,128]{1,0:T(8,128)(2,1)S(1)} %slice.37), channel_id=1, source_target_pairs={{0,1},{2,3},{4,5},{6,7},{1,0},{3,2},{5,4},{7,6},{8,9},{10,11},{12,... | collective-permute-start | bytes 2371592 | tf_op jit(solution)/shard_map/ppermute | solution.py:294
  6.9 11.1 %collective-permute-done.1.refs_2_ = bf16[3104,128]{1,0:T(8,128)(2,1)S(1)} collective-permute-done((bf16[3104,128]{1,0:T(8,128)(2,1)S(1)}, bf16[3104,128]{1,0:T(8,128)(2,1)S(1)}, u32[]{:S(2)}, u32[]{:S(2)}) %collective-permute-start.1) | collective-permute-done | bytes 794656 | tf_op jit(solution)/shard_map/ppermute | solution.py:294
  18.0 0.1 slice.36
  18.0 1.3 %collective-permute-start.2 = (bf16[3088,128]{1,0:T(8,128)(2,1)S(1)}, bf16[3088,128]{1,0:T(8,128)(2,1)S(1)}, u32[]{:S(2)}, u32[]{:S(2)}) collective-permute-start(bf16[3088,128]{1,0:T(8,128)(2,1)S(1)} %slice.36), channel_id=1, source_target_pairs={{2,3},{4,5},{6,7},{1,0},{3,2},{5,4},{10,11},{12,13},{14,15},{9,8},... | collective-permute-start | bytes 2371592 | tf_op jit(solution)/shard_map/ppermute | solution.py:294
  19.3 0.0 collective-permute-done.7.refs_1_
  19.3 0.7 %collective-permute-start.8 = (bf16[3104,128]{1,0:T(8,128)(2,1)S(1)}, bf16[3104,128]{1,0:T(8,128)(2,1)S(1)}, u32[]{:S(2)}, u32[]{:S(2)}) collective-permute-start(bf16[3104,128]{1,0:T(8,128)(2,1)S(1)} %collective-permute-done.1.refs_2_), channel_id=1, source_target_pairs={{2,4},{4,6},{3,1},{5,3},{10,12},{12,14},{11,9},{13,11},{18,20},{20... | collective-permute-start | bytes 2383880 | tf_op jit(solution)/shard_map/ppermute | solution.py:294
  20.0 0.0 collective-permute-done.refs_3_
  20.1 8.9 %collective-permute-done.3.refs_11_ = bf16[1024,512]{1,0:T(8,128)(2,1)S(1)} collective-permute-done((bf16[1024,512]{1,0:T(8,128)(2,1)}, bf16[1024,512]{1,0:T(8,128)(2,1)S(1)}, u32[]{:S(2)}, u32[]{:S(2)}) %collective-permute-start.3) | collective-permute-done | bytes 1048608 | tf_op jit(solution)/shard_map/ppermute | solution.py:294
  28.9 0.0 collective-permute-done.4.refs_12_
  28.9 0.0 collective-permute-done.2.refs_4_
  28.9 0.7 %collective-permute-start.5 = (bf16[3104,128]{1,0:T(8,128)(2,1)S(1)}, bf16[3104,128]{1,0:T(8,128)(2,1)S(1)}, u32[]{:S(2)}, u32[]{:S(2)}) collective-permute-start(bf16[3104,128]{1,0:T(8,128)(2,1)S(1)} %collective-permute-done.refs_3_), channel_id=1, source_target_pairs={{2,4},{4,6},{3,1},{5,3},{10,12},{12,14},{11,9},{13,11},{18,20},{20... | collective-permute-start | bytes 2383880 | tf_op jit(solution)/shard_map/ppermute | solution.py:294
  29.7 0.0 copy-start
  29.7 0.3 collective-permute-start.12
  30.0 1.3 %collective-permute-start.14 = (bf16[512,512]{1,0:T(8,128)(2,1)S(1)}, bf16[512,512]{1,0:T(8,128)(2,1)S(1)}, u32[]{:S(2)}, u32[]{:S(2)}) collective-permute-start(bf16[512,512]{1,0:T(8,128)(2,1)S(1)} %slice.42), channel_id=1, source_target_pairs={{0,8},{8,0},{16,24},{24,16},{1,9},{9,1},{17,25},{25,17},{2,10},{10... | collective-permute-start | bytes 1572872 | tf_op jit(solution)/shard_map/ppermute | solution.py:294
  31.3 0.0 collective-permute-done.8.refs_6_
  31.3 0.7 %collective-permute-start.9 = (bf16[3104,128]{1,0:T(8,128)(2,1)S(1)}, bf16[3104,128]{1,0:T(8,128)(2,1)S(1)}, u32[]{:S(2)}, u32[]{:S(2)}) collective-permute-start(bf16[3104,128]{1,0:T(8,128)(2,1)S(1)} %collective-permute-done.8.refs_6_), channel_id=1, source_target_pairs={{4,6},{3,1},{12,14},{11,9},{20,22},{19,17},{28,30},{27,25}} | collective-permute-start | bytes 2383880 | tf_op jit(solution)/shard_map/ppermute | solution.py:294
  32.0 0.1 slice.38
  32.1 1.3 %collective-permute-start.10 = (bf16[3088,128]{1,0:T(8,128)(2,1)S(1)}, bf16[3088,128]{1,0:T(8,128)(2,1)S(1)}, u32[]{:S(2)}, u32[]{:S(2)}) collective-permute-start(bf16[3088,128]{1,0:T(8,128)(2,1)S(1)} %slice.38), channel_id=1, source_target_pairs={{2,3},{4,5},{6,7},{1,0},{3,2},{5,4},{10,11},{12,13},{14,15},{9,8},... | collective-permute-start | bytes 2371592 | tf_op jit(solution)/shard_map/ppermute | solution.py:294
  33.4 0.1 slice.39
  33.4 0.0 collective-permute-done.5.refs_7_
  33.4 1.3 %collective-permute-start.11 = (bf16[3088,128]{1,0:T(8,128)(2,1)S(1)}, bf16[3088,128]{1,0:T(8,128)(2,1)S(1)}, u32[]{:S(2)}, u32[]{:S(2)}) collective-permute-start(bf16[3088,128]{1,0:T(8,128)(2,1)S(1)} %slice.39), channel_id=1, source_target_pairs={{4,5},{6,7},{1,0},{3,2},{12,13},{14,15},{9,8},{11,10},{20,21},{22,... | collective-permute-start | bytes 2371592 | tf_op jit(solution)/shard_map/ppermute | solution.py:294
  34.7 0.1 slice.40
  34.8 6.9 %collective-permute-done.12.refs_13_ = bf16[512,512]{1,0:T(8,128)(2,1)S(1)} collective-permute-done((bf16[512,512]{1,0:T(8,128)(2,1)S(1)}, bf16[512,512]{1,0:T(8,128)(2,1)S(1)}, u32[]{:S(2)}, u32[]{:S(2)}) %collective-permute-start.12) | collective-permute-done | bytes 524320 | tf_op jit(solution)/shard_map/ppermute | solution.py:294
  41.7 1.3 %collective-permute-start.13 = (bf16[3088,128]{1,0:T(8,128)(2,1)S(1)}, bf16[3088,128]{1,0:T(8,128)(2,1)S(1)}, u32[]{:S(2)}, u32[]{:S(2)}) collective-permute-start(bf16[3088,128]{1,0:T(8,128)(2,1)S(1)} %slice.40), channel_id=1, source_target_pairs={{4,5},{6,7},{1,0},{3,2},{12,13},{14,15},{9,8},{11,10},{20,21},{22,... | collective-permute-start | bytes 2371592 | tf_op jit(solution)/shard_map/ppermute | solution.py:294
  42.9 0.0 collective-permute-done.14.refs_14_
  43.0 0.7 %collective-permute-start.6 = (bf16[3104,128]{1,0:T(8,128)(2,1)S(1)}, bf16[3104,128]{1,0:T(8,128)(2,1)S(1)}, u32[]{:S(2)}, u32[]{:S(2)}) collective-permute-start(bf16[3104,128]{1,0:T(8,128)(2,1)S(1)} %collective-permute-done.5.refs_7_), channel_id=1, source_target_pairs={{4,6},{3,1},{12,14},{11,9},{20,22},{19,17},{28,30},{27,25}} | collective-permute-start | bytes 2383880 | tf_op jit(solution)/shard_map/ppermute | solution.py:294
  43.7 0.0 collective-permute-done.10.refs_5_
  43.7 6.1 %collective-permute-done.11.refs_8_ = bf16[3088,128]{1,0:T(8,128)(2,1)S(1)} collective-permute-done((bf16[3088,128]{1,0:T(8,128)(2,1)S(1)}, bf16[3088,128]{1,0:T(8,128)(2,1)S(1)}, u32[]{:S(2)}, u32[]{:S(2)}) %collective-permute-start.11) | collective-permute-done | bytes 790560 | tf_op jit(solution)/shard_map/ppermute | solution.py:294
  49.8 1.4 %collective-permute-done.13.refs_9_ = bf16[3088,128]{1,0:T(8,128)(2,1)S(1)} collective-permute-done((bf16[3088,128]{1,0:T(8,128)(2,1)S(1)}, bf16[3088,128]{1,0:T(8,128)(2,1)S(1)}, u32[]{:S(2)}, u32[]{:S(2)}) %collective-permute-start.13) | collective-permute-done | bytes 790560 | tf_op jit(solution)/shard_map/ppermute | solution.py:294
  51.2 0.0 copy-done
  51.2 8.8 %near.1 = (f32[1536,512]{1,0:T(8,128)S(1)}, bf16[1024,512]{1,0:T(8,128)(2,1)S(1)}) custom-call(s32[32]{0:T(128)} %order_ref.1, bf16[3104,128]{1,0:T(8,128)(2,1)S(1)} %pack.1.refs_0_, bf16[3088,128]{1,0:T(8,128)(2,1)S(1)} %collective-permute-done.7.refs_1_, bf16[3104,128]{1,0:T(8,128)(2,1)S(1)} %collective-permute-done.1.refs_2_, ...), custom_call_target="tpu_custom_call" | custom-call | tf_op jit(solution)/shard_map/near/pallas_call | solution.py:190
  60.0 0.0 collective-permute-done.9.mine
  60.1 0.1 slice.35
  60.1 1.3 %collective-permute-start.16 = (bf16[3088,128]{1,0:T(8,128)(2,1)S(1)}, bf16[3088,128]{1,0:T(8,128)(2,1)S(1)}, u32[]{:S(2)}, u32[]{:S(2)}) collective-permute-start(bf16[3088,128]{1,0:T(8,128)(2,1)S(1)} %slice.35), channel_id=1, source_target_pairs={{6,7},{1,0},{14,15},{9,8},{22,23},{17,16},{30,31},{25,24}} | collective-permute-start | bytes 2371592 | tf_op jit(solution)/shard_map/ppermute | solution.py:294
  61.4 0.0 collective-permute-done.6.mine
  61.4 0.1 slice.34
  61.5 1.3 %collective-permute-start.15 = (bf16[3088,128]{1,0:T(8,128)(2,1)S(1)}, bf16[3088,128]{1,0:T(8,128)(2,1)S(1)}, u32[]{:S(2)}, u32[]{:S(2)}) collective-permute-start(bf16[3088,128]{1,0:T(8,128)(2,1)S(1)} %slice.34), channel_id=1, source_target_pairs={{6,7},{1,0},{14,15},{9,8},{22,23},{17,16},{30,31},{25,24}} | collective-permute-start | bytes 2371592 | tf_op jit(solution)/shard_map/ppermute | solution.py:294
  62.8 1.5 %collective-permute-done.16.other = bf16[3088,128]{1,0:T(8,128)(2,1)S(1)} collective-permute-done((bf16[3088,128]{1,0:T(8,128)(2,1)S(1)}, bf16[3088,128]{1,0:T(8,128)(2,1)S(1)}, u32[]{:S(2)}, u32[]{:S(2)}) %collective-permute-start.16) | collective-permute-done | bytes 790560 | tf_op jit(solution)/shard_map/ppermute | solution.py:294
  64.3 1.7 %far.2.total_in = f32[1536,512]{1,0:T(8,128)S(1)} custom-call(bf16[3104,128]{1,0:T(8,128)(2,1)S(1)} %collective-permute-done.9.mine, bf16[3088,128]{1,0:T(8,128)(2,1)S(1)} %collective-permute-done.16.other, bf16[1024,512]{1,0:T(8,128)(2,1)S(1)} %get-tuple-element.22.far_rows, f32[1536,512]{1,0:T(8,128)S(1)} %get-tuple-element.24.total_in), custom_call_target="tpu_custom_call", output_to_operand_aliasing={{}: (3, {})} | custom-call | flops 805306368 | bytes 8388608 | tf_op jit(solution)/shard_map/far/pallas_call | solution.py:254
  66.0 0.9 %collective-permute-done.15.other = bf16[3088,128]{1,0:T(8,128)(2,1)S(1)} collective-permute-done((bf16[3088,128]{1,0:T(8,128)(2,1)S(1)}, bf16[3088,128]{1,0:T(8,128)(2,1)S(1)}, u32[]{:S(2)}, u32[]{:S(2)}) %collective-permute-start.15) | collective-permute-done | bytes 790560 | tf_op jit(solution)/shard_map/ppermute | solution.py:294
  66.9 2.7 %far.3 = f32[1536,512]{1,0:T(8,128)} custom-call(bf16[3104,128]{1,0:T(8,128)(2,1)S(1)} %collective-permute-done.6.mine, bf16[3088,128]{1,0:T(8,128)(2,1)S(1)} %collective-permute-done.15.other, bf16[1024,512]{1,0:T(8,128)(2,1)S(1)} %get-tuple-element.22.far_rows, f32[1536,512]{1,0:T(8,128)S(1)} %far.2.total_in), custom_call_target="tpu_custom_call" | custom-call | flops 805306368 | bytes 8388608 | tf_op jit(solution)/shard_map/far/pallas_call | solution.py:254
  (2 shorter events, 0.1 us)
Async XLA Ops:
  1.6 16.3 %collective-permute-start.1 = (bf16[3104,128]{1,0:T(8,128)(2,1)S(1)}, bf16[3104,128]{1,0:T(8,128)(2,1)S(1)}, u32[]{:S(2)}, u32[]{:S(2)}) collective-permute-start(bf16[3104,128]{1,0:T(8,128)(2,1)S(1)} %pack.1.refs_0_), channel_id=1, source_target_pairs={{0,2},{2,4},{4,6},{3,1},{5,3},{7,5},{8,10},{10,12},{12,14},{11,9},... | collective-permute-start | bytes 2383880 | tf_op jit(solution)/shard_map/ppermute | solution.py:294
  3.8 25.2 %collective-permute-start.3 = (bf16[1024,512]{1,0:T(8,128)(2,1)}, bf16[1024,512]{1,0:T(8,128)(2,1)S(1)}, u32[]{:S(2)}, u32[]{:S(2)}) collective-permute-start(bf16[1024,512]{1,0:T(8,128)(2,1)} %refs_10_.1), channel_id=1, source_target_pairs={{0,8},{8,0},{16,24},{24,16},{1,9},{9,1},{17,25},{25,17},{2,10},{10... | collective-permute-start | bytes 3145736 | tf_op jit(solution)/shard_map/ppermute | solution.py:294
  4.1 24.8 %collective-permute-start.4 = (bf16[1024,512]{1,0:T(8,128)(2,1)}, bf16[1024,512]{1,0:T(8,128)(2,1)S(1)}, u32[]{:S(2)}, u32[]{:S(2)}) collective-permute-start(bf16[1024,512]{1,0:T(8,128)(2,1)} %refs_10_.1), channel_id=1, source_target_pairs={{0,16},{8,24},{16,0},{24,8},{1,17},{9,25},{17,1},{25,9},{2,18},{10... | collective-permute-start | bytes 3145736 | tf_op jit(solution)/shard_map/ppermute | solution.py:294
  4.3 15.7 %collective-permute-start = (bf16[3104,128]{1,0:T(8,128)(2,1)S(1)}, bf16[3104,128]{1,0:T(8,128)(2,1)S(1)}, u32[]{:S(2)}, u32[]{:S(2)}) collective-permute-start(bf16[3104,128]{1,0:T(8,128)(2,1)S(1)} %pack.1.refs_0_), channel_id=1, source_target_pairs={{1,2},{3,4},{5,6},{2,1},{4,3},{6,5},{9,10},{11,12},{13,14},{10,9},... | collective-permute-start | bytes 2383880 | tf_op jit(solution)/shard_map/ppermute | solution.py:294
  5.1 14.2 %collective-permute-start.7 = (bf16[3088,128]{1,0:T(8,128)(2,1)S(1)}, bf16[3088,128]{1,0:T(8,128)(2,1)S(1)}, u32[]{:S(2)}, u32[]{:S(2)}) collective-permute-start(bf16[3088,128]{1,0:T(8,128)(2,1)S(1)} %slice.37), channel_id=1, source_target_pairs={{0,1},{2,3},{4,5},{6,7},{1,0},{3,2},{5,4},{7,6},{8,9},{10,11},{12,... | collective-permute-start | bytes 2371592 | tf_op jit(solution)/shard_map/ppermute | solution.py:294
  18.0 10.9 %collective-permute-start.2 = (bf16[3088,128]{1,0:T(8,128)(2,1)S(1)}, bf16[3088,128]{1,0:T(8,128)(2,1)S(1)}, u32[]{:S(2)}, u32[]{:S(2)}) collective-permute-start(bf16[3088,128]{1,0:T(8,128)(2,1)S(1)} %slice.36), channel_id=1, source_target_pairs={{2,3},{4,5},{6,7},{1,0},{3,2},{5,4},{10,11},{12,13},{14,15},{9,8},... | collective-permute-start | bytes 2371592 | tf_op jit(solution)/shard_map/ppermute | solution.py:294
  19.3 12.0 %collective-permute-start.8 = (bf16[3104,128]{1,0:T(8,128)(2,1)S(1)}, bf16[3104,128]{1,0:T(8,128)(2,1)S(1)}, u32[]{:S(2)}, u32[]{:S(2)}) collective-permute-start(bf16[3104,128]{1,0:T(8,128)(2,1)S(1)} %collective-permute-done.1.refs_2_), channel_id=1, source_target_pairs={{2,4},{4,6},{3,1},{5,3},{10,12},{12,14},{11,9},{13,11},{18,20},{20... | collective-permute-start | bytes 2383880 | tf_op jit(solution)/shard_map/ppermute | solution.py:294
  28.9 4.5 %collective-permute-start.5 = (bf16[3104,128]{1,0:T(8,128)(2,1)S(1)}, bf16[3104,128]{1,0:T(8,128)(2,1)S(1)}, u32[]{:S(2)}, u32[]{:S(2)}) collective-permute-start(bf16[3104,128]{1,0:T(8,128)(2,1)S(1)} %collective-permute-done.refs_3_), channel_id=1, source_target_pairs={{2,4},{4,6},{3,1},{5,3},{10,12},{12,14},{11,9},{13,11},{18,20},{20... | collective-permute-start | bytes 2383880 | tf_op jit(solution)/shard_map/ppermute | solution.py:294
  29.7 21.5 %copy-start = (bf16[1024,512]{1,0:T(8,128)(2,1)S(1)}, bf16[1024,512]{1,0:T(8,128)(2,1)}, u32[]{:S(2)}) copy-start(bf16[1024,512]{1,0:T(8,128)(2,1)} %refs_10_.1) | copy-start | bytes 3145732
  29.7 12.0 %collective-permute-start.12 = (bf16[512,512]{1,0:T(8,128)(2,1)S(1)}, bf16[512,512]{1,0:T(8,128)(2,1)S(1)}, u32[]{:S(2)}, u32[]{:S(2)}) collective-permute-start(bf16[512,512]{1,0:T(8,128)(2,1)S(1)} %slice.41), channel_id=1, source_target_pairs={{0,16},{8,24},{16,0},{24,8},{1,17},{9,25},{17,1},{25,9},{2,18},{10... | collective-permute-start | bytes 1572872 | tf_op jit(solution)/shard_map/ppermute | solution.py:294
  30.0 12.9 %collective-permute-start.14 = (bf16[512,512]{1,0:T(8,128)(2,1)S(1)}, bf16[512,512]{1,0:T(8,128)(2,1)S(1)}, u32[]{:S(2)}, u32[]{:S(2)}) collective-permute-start(bf16[512,512]{1,0:T(8,128)(2,1)S(1)} %slice.42), channel_id=1, source_target_pairs={{0,8},{8,0},{16,24},{24,16},{1,9},{9,1},{17,25},{25,17},{2,10},{10... | collective-permute-start | bytes 1572872 | tf_op jit(solution)/shard_map/ppermute | solution.py:294
  31.3 28.8 %collective-permute-start.9 = (bf16[3104,128]{1,0:T(8,128)(2,1)S(1)}, bf16[3104,128]{1,0:T(8,128)(2,1)S(1)}, u32[]{:S(2)}, u32[]{:S(2)}) collective-permute-start(bf16[3104,128]{1,0:T(8,128)(2,1)S(1)} %collective-permute-done.8.refs_6_), channel_id=1, source_target_pairs={{4,6},{3,1},{12,14},{11,9},{20,22},{19,17},{28,30},{27,25}} | collective-permute-start | bytes 2383880 | tf_op jit(solution)/shard_map/ppermute | solution.py:294
  32.1 11.6 %collective-permute-start.10 = (bf16[3088,128]{1,0:T(8,128)(2,1)S(1)}, bf16[3088,128]{1,0:T(8,128)(2,1)S(1)}, u32[]{:S(2)}, u32[]{:S(2)}) collective-permute-start(bf16[3088,128]{1,0:T(8,128)(2,1)S(1)} %slice.38), channel_id=1, source_target_pairs={{2,3},{4,5},{6,7},{1,0},{3,2},{5,4},{10,11},{12,13},{14,15},{9,8},... | collective-permute-start | bytes 2371592 | tf_op jit(solution)/shard_map/ppermute | solution.py:294
  33.4 16.4 %collective-permute-start.11 = (bf16[3088,128]{1,0:T(8,128)(2,1)S(1)}, bf16[3088,128]{1,0:T(8,128)(2,1)S(1)}, u32[]{:S(2)}, u32[]{:S(2)}) collective-permute-start(bf16[3088,128]{1,0:T(8,128)(2,1)S(1)} %slice.39), channel_id=1, source_target_pairs={{4,5},{6,7},{1,0},{3,2},{12,13},{14,15},{9,8},{11,10},{20,21},{22,... | collective-permute-start | bytes 2371592 | tf_op jit(solution)/shard_map/ppermute | solution.py:294
  41.7 9.6 %collective-permute-start.13 = (bf16[3088,128]{1,0:T(8,128)(2,1)S(1)}, bf16[3088,128]{1,0:T(8,128)(2,1)S(1)}, u32[]{:S(2)}, u32[]{:S(2)}) collective-permute-start(bf16[3088,128]{1,0:T(8,128)(2,1)S(1)} %slice.40), channel_id=1, source_target_pairs={{4,5},{6,7},{1,0},{3,2},{12,13},{14,15},{9,8},{11,10},{20,21},{22,... | collective-permute-start | bytes 2371592 | tf_op jit(solution)/shard_map/ppermute | solution.py:294
  43.0 18.5 %collective-permute-start.6 = (bf16[3104,128]{1,0:T(8,128)(2,1)S(1)}, bf16[3104,128]{1,0:T(8,128)(2,1)S(1)}, u32[]{:S(2)}, u32[]{:S(2)}) collective-permute-start(bf16[3104,128]{1,0:T(8,128)(2,1)S(1)} %collective-permute-done.5.refs_7_), channel_id=1, source_target_pairs={{4,6},{3,1},{12,14},{11,9},{20,22},{19,17},{28,30},{27,25}} | collective-permute-start | bytes 2383880 | tf_op jit(solution)/shard_map/ppermute | solution.py:294
  60.1 4.2 %collective-permute-start.16 = (bf16[3088,128]{1,0:T(8,128)(2,1)S(1)}, bf16[3088,128]{1,0:T(8,128)(2,1)S(1)}, u32[]{:S(2)}, u32[]{:S(2)}) collective-permute-start(bf16[3088,128]{1,0:T(8,128)(2,1)S(1)} %slice.35), channel_id=1, source_target_pairs={{6,7},{1,0},{14,15},{9,8},{22,23},{17,16},{30,31},{25,24}} | collective-permute-start | bytes 2371592 | tf_op jit(solution)/shard_map/ppermute | solution.py:294
  61.5 5.4 %collective-permute-start.15 = (bf16[3088,128]{1,0:T(8,128)(2,1)S(1)}, bf16[3088,128]{1,0:T(8,128)(2,1)S(1)}, u32[]{:S(2)}, u32[]{:S(2)}) collective-permute-start(bf16[3088,128]{1,0:T(8,128)(2,1)S(1)} %slice.34), channel_id=1, source_target_pairs={{6,7},{1,0},{14,15},{9,8},{22,23},{17,16},{30,31},{25,24}} | collective-permute-start | bytes 2371592 | tf_op jit(solution)/shard_map/ppermute | solution.py:294

commit v2 on v1

--- a/solution.py
+++ b/solution.py
@@ -11,6 +11,7 @@
 CAP = 24
 META = 16
 ROWS = 512
+LAST_ROWS = 256
 LANES = 128
 SWAP = CAP * TILE + META
 BLOCK = SWAP + META
@@ -71,10 +72,14 @@
         for k in range(col_tiles):
             keep = mask_ref[k, i] != 0
 
-            @pl.when(keep)
-            def _(i=i, k=k, slot=slot):
+            def store(i=i, k=k, slot=slot):
                 to = pl.ds(pl.multiple_of(slot * TILE, TILE), TILE)
                 packed[to] = amplitudes[pl.ds(i * TILE, TILE), pl.ds(k * TILE, TILE)]
+
+            if i * col_tiles + k < CAP:
+                store()
+            else:
+                pl.when(keep)(store)
 
             places = jnp.where(lane == i * col_tiles + k, jnp.where(keep, slot, CAP), places)
             slot = slot + keep.astype(jnp.int32)
@@ -103,12 +108,12 @@
     )(in_hbm(mask.T), in_hbm(amplitudes))
 
 
-def unpacked(places_ref, table, rows, packed, col_tiles):
+def unpacked(places_ref, table, rows, packed, col_tiles, height=ROWS):
     lines = []
-    for i in range(ROWS // TILE):
+    for i in range(height // TILE):
         line = []
         for k in range(col_tiles):
-            place = places_ref[table, 0, (rows * (ROWS // TILE) + i) * col_tiles + k]
+            place = places_ref[table, 0, (rows * (height // TILE) + i) * col_tiles + k]
             at = pl.multiple_of(jnp.minimum(place, CAP - 1) * TILE, TILE)
             tile = packed[pl.ds(at, TILE)]
             line.append(jnp.where(place < CAP, tile, jnp.zeros_like(tile)))
@@ -209,10 +214,11 @@
     col = lax.axis_index("col")
     chip, core = col // 2, col % 2
     depth = far_rows.shape[0] // 2
-    outs = [None] * (total.shape[0] // ROWS)
+    height = LAST_ROWS if last else ROWS
+    outs = [None] * (total.shape[0] // height)
     if last:
         for m in range(len(outs)):
-            at = pl.ds(m * ROWS, ROWS)
+            at = pl.ds(m * height, height)
             outs[m] = pltpu.make_async_copy(total.at[at], total_out.at[at], refs[3].at[m])
 
     for ref, stream in ((mine, core), (other, 1 - core)):
@@ -226,8 +232,9 @@
             right = far_rows[pl.ds(start, depth)]
             copy.wait()
             for m, out in enumerate(outs):
-                at = pl.ds(m * ROWS, ROWS)
-                total[at] = total_in[at] + dot(unpacked(places, 0, m, ref, depth // TILE), right)
+                at = pl.ds(m * height, height)
+                left = unpacked(places, 0, m, ref, depth // TILE, height)
+                total[at] = total_in[at] + dot(left, right)
                 if last:
                     out.start()
 
@@ -236,7 +243,7 @@
         @pl.when((chip != 0) & (chip != chips - 1))
         def _():
             for m, out in enumerate(outs):
-                at = pl.ds(m * ROWS, ROWS)
+                at = pl.ds(m * height, height)
                 total[at] = total_in[at]
                 out.start()
 
@@ -250,7 +257,7 @@
     scratch = [((8, LANES), jnp.int32)]
     if last:
         scratch.insert(0, (shape, jnp.float32))
-    sems = [pltpu.SemaphoreType.DMA((local_rows // ROWS,))] if last else []
+    sems = [pltpu.SemaphoreType.DMA((local_rows // LAST_ROWS,))] if last else []
     return pl.pallas_call(
         functools.partial(far_kernel, chips, block, last),
         out_shape=(pltpu.HBM if last else pltpu.VMEM)(shape, jnp.float32),

time: 70 us -> 69.9 us (level)
  no operation moved by 1% of the time
where the time goes in v2:
time: 69.9 us; the launch traced here: 69.5 us
  waiting for transfers between devices  36.8 us (53%)
  starting transfers between devices  17.3 us (25%)
  Pallas kernels  14.7 us (21%)
    ppermute x17, waiting for transfers between devices, send(): return lax.ppermute(after(chunk, others), axis, perm)  36.8 us
    ppermute x17, starting transfers between devices, send(): return lax.ppermute(after(chunk, others), axis, perm)  17.3 us
    pallas_call x1, Pallas kernels, near(): pl.pallas_call(functools.partial(near_kernel, chips, row_devices, steps,...  8.8 us
    pallas_call x2, Pallas kernels, far(): pl.pallas_call(functools.partial(far_kernel, chips, block, last), out_sha...  4.32 us
    pallas_call x1, Pallas kernels, pack(): pl.pallas_call(pack_kernel, out_shape=pltpu.VMEM(shape, dtype), in_specs=...  1.61 us
  transfers between devices with their start and end apart: 17, of which 7 were waited for; matrix products, arithmetic and copies ran while one was open for 1% of the time, Pallas kernels for 15%

profile of v2, /device:TPU:31, one launch (start us, length us, event | category | flops | bytes accessed | tf_op | source)
XLA Modules:
  0.0 69.5 jit_solution(15413710427165004921)
XLA Ops:
  0.0 1.6 %pack.1.refs_0_ = bf16[3104,128]{1,0:T(8,128)(2,1)S(1)} custom-call(s32[4,12]{1,0:T(4,128)} %bitcast.1, bf16[1536,512]{1,0:T(8,128)(2,1)} %amplitudes_ref.1), custom_call_target="tpu_custom_call" | custom-call | bytes 2383872 | tf_op jit(solution)/shard_map/pack/pallas_call | solution.py:92
  1.6 2.1 %collective-permute-start.1 = (bf16[3104,128]{1,0:T(8,128)(2,1)S(1)}, bf16[3104,128]{1,0:T(8,128)(2,1)S(1)}, u32[]{:S(2)}, u32[]{:S(2)}) collective-permute-start(bf16[3104,128]{1,0:T(8,128)(2,1)S(1)} %pack.1.refs_0_), channel_id=1, source_target_pairs={{0,2},{2,4},{4,6},{3,1},{5,3},{7,5},{8,10},{10,12},{12,14},{11,9},... | collective-permute-start | bytes 2383880 | tf_op jit(solution)/shard_map/ppermute | solution.py:301
  3.7 0.3 collective-permute-start.3
  4.1 0.2 collective-permute-start.4
  4.3 0.7 %collective-permute-start = (bf16[3104,128]{1,0:T(8,128)(2,1)S(1)}, bf16[3104,128]{1,0:T(8,128)(2,1)S(1)}, u32[]{:S(2)}, u32[]{:S(2)}) collective-permute-start(bf16[3104,128]{1,0:T(8,128)(2,1)S(1)} %pack.1.refs_0_), channel_id=1, source_target_pairs={{1,2},{3,4},{5,6},{2,1},{4,3},{6,5},{9,10},{11,12},{13,14},{10,9},... | collective-permute-start | bytes 2383880 | tf_op jit(solution)/shard_map/ppermute | solution.py:301
  5.0 0.1 slice.37
  5.1 1.8 %collective-permute-start.7 = (bf16[3088,128]{1,0:T(8,128)(2,1)S(1)}, bf16[3088,128]{1,0:T(8,128)(2,1)S(1)}, u32[]{:S(2)}, u32[]{:S(2)}) collective-permute-start(bf16[3088,128]{1,0:T(8,128)(2,1)S(1)} %slice.37), channel_id=1, source_target_pairs={{0,1},{2,3},{4,5},{6,7},{1,0},{3,2},{5,4},{7,6},{8,9},{10,11},{12,... | collective-permute-start | bytes 2371592 | tf_op jit(solution)/shard_map/ppermute | solution.py:301
  6.9 11.1 %collective-permute-done.1.refs_2_ = bf16[3104,128]{1,0:T(8,128)(2,1)S(1)} collective-permute-done((bf16[3104,128]{1,0:T(8,128)(2,1)S(1)}, bf16[3104,128]{1,0:T(8,128)(2,1)S(1)}, u32[]{:S(2)}, u32[]{:S(2)}) %collective-permute-start.1) | collective-permute-done | bytes 794656 | tf_op jit(solution)/shard_map/ppermute | solution.py:301
  17.9 0.1 slice.36
  18.0 1.3 %collective-permute-start.2 = (bf16[3088,128]{1,0:T(8,128)(2,1)S(1)}, bf16[3088,128]{1,0:T(8,128)(2,1)S(1)}, u32[]{:S(2)}, u32[]{:S(2)}) collective-permute-start(bf16[3088,128]{1,0:T(8,128)(2,1)S(1)} %slice.36), channel_id=1, source_target_pairs={{2,3},{4,5},{6,7},{1,0},{3,2},{5,4},{10,11},{12,13},{14,15},{9,8},... | collective-permute-start | bytes 2371592 | tf_op jit(solution)/shard_map/ppermute | solution.py:301
  19.3 0.0 collective-permute-done.7.refs_1_
  19.3 0.7 %collective-permute-start.8 = (bf16[3104,128]{1,0:T(8,128)(2,1)S(1)}, bf16[3104,128]{1,0:T(8,128)(2,1)S(1)}, u32[]{:S(2)}, u32[]{:S(2)}) collective-permute-start(bf16[3104,128]{1,0:T(8,128)(2,1)S(1)} %collective-permute-done.1.refs_2_), channel_id=1, source_target_pairs={{2,4},{4,6},{3,1},{5,3},{10,12},{12,14},{11,9},{13,11},{18,20},{20... | collective-permute-start | bytes 2383880 | tf_op jit(solution)/shard_map/ppermute | solution.py:301
  20.0 0.0 collective-permute-done.refs_3_
  20.0 8.9 %collective-permute-done.3.refs_11_ = bf16[1024,512]{1,0:T(8,128)(2,1)S(1)} collective-permute-done((bf16[1024,512]{1,0:T(8,128)(2,1)}, bf16[1024,512]{1,0:T(8,128)(2,1)S(1)}, u32[]{:S(2)}, u32[]{:S(2)}) %collective-permute-start.3) | collective-permute-done | bytes 1048608 | tf_op jit(solution)/shard_map/ppermute | solution.py:301
  28.9 0.0 collective-permute-done.4.refs_12_
  28.9 0.0 collective-permute-done.2.refs_4_
  28.9 0.7 %collective-permute-start.5 = (bf16[3104,128]{1,0:T(8,128)(2,1)S(1)}, bf16[3104,128]{1,0:T(8,128)(2,1)S(1)}, u32[]{:S(2)}, u32[]{:S(2)}) collective-permute-start(bf16[3104,128]{1,0:T(8,128)(2,1)S(1)} %collective-permute-done.refs_3_), channel_id=1, source_target_pairs={{2,4},{4,6},{3,1},{5,3},{10,12},{12,14},{11,9},{13,11},{18,20},{20... | collective-permute-start | bytes 2383880 | tf_op jit(solution)/shard_map/ppermute | solution.py:301
  29.7 0.0 copy-start
  29.7 0.3 collective-permute-start.12
  30.0 1.3 %collective-permute-start.14 = (bf16[512,512]{1,0:T(8,128)(2,1)S(1)}, bf16[512,512]{1,0:T(8,128)(2,1)S(1)}, u32[]{:S(2)}, u32[]{:S(2)}) collective-permute-start(bf16[512,512]{1,0:T(8,128)(2,1)S(1)} %slice.42), channel_id=1, source_target_pairs={{0,8},{8,0},{16,24},{24,16},{1,9},{9,1},{17,25},{25,17},{2,10},{10... | collective-permute-start | bytes 1572872 | tf_op jit(solution)/shard_map/ppermute | solution.py:301
  31.3 0.0 collective-permute-done.8.refs_6_
  31.3 0.7 %collective-permute-start.9 = (bf16[3104,128]{1,0:T(8,128)(2,1)S(1)}, bf16[3104,128]{1,0:T(8,128)(2,1)S(1)}, u32[]{:S(2)}, u32[]{:S(2)}) collective-permute-start(bf16[3104,128]{1,0:T(8,128)(2,1)S(1)} %collective-permute-done.8.refs_6_), channel_id=1, source_target_pairs={{4,6},{3,1},{12,14},{11,9},{20,22},{19,17},{28,30},{27,25}} | collective-permute-start | bytes 2383880 | tf_op jit(solution)/shard_map/ppermute | solution.py:301
  32.0 0.1 slice.38
  32.0 1.3 %collective-permute-start.10 = (bf16[3088,128]{1,0:T(8,128)(2,1)S(1)}, bf16[3088,128]{1,0:T(8,128)(2,1)S(1)}, u32[]{:S(2)}, u32[]{:S(2)}) collective-permute-start(bf16[3088,128]{1,0:T(8,128)(2,1)S(1)} %slice.38), channel_id=1, source_target_pairs={{2,3},{4,5},{6,7},{1,0},{3,2},{5,4},{10,11},{12,13},{14,15},{9,8},... | collective-permute-start | bytes 2371592 | tf_op jit(solution)/shard_map/ppermute | solution.py:301
  33.3 0.1 slice.39
  33.4 0.0 collective-permute-done.5.refs_7_
  33.4 1.3 %collective-permute-start.11 = (bf16[3088,128]{1,0:T(8,128)(2,1)S(1)}, bf16[3088,128]{1,0:T(8,128)(2,1)S(1)}, u32[]{:S(2)}, u32[]{:S(2)}) collective-permute-start(bf16[3088,128]{1,0:T(8,128)(2,1)S(1)} %slice.39), channel_id=1, source_target_pairs={{4,5},{6,7},{1,0},{3,2},{12,13},{14,15},{9,8},{11,10},{20,21},{22,... | collective-permute-start | bytes 2371592 | tf_op jit(solution)/shard_map/ppermute | solution.py:301
  34.7 0.1 slice.40
  34.8 6.9 %collective-permute-done.12.refs_13_ = bf16[512,512]{1,0:T(8,128)(2,1)S(1)} collective-permute-done((bf16[512,512]{1,0:T(8,128)(2,1)S(1)}, bf16[512,512]{1,0:T(8,128)(2,1)S(1)}, u32[]{:S(2)}, u32[]{:S(2)}) %collective-permute-start.12) | collective-permute-done | bytes 524320 | tf_op jit(solution)/shard_map/ppermute | solution.py:301
  41.6 1.3 %collective-permute-start.13 = (bf16[3088,128]{1,0:T(8,128)(2,1)S(1)}, bf16[3088,128]{1,0:T(8,128)(2,1)S(1)}, u32[]{:S(2)}, u32[]{:S(2)}) collective-permute-start(bf16[3088,128]{1,0:T(8,128)(2,1)S(1)} %slice.40), channel_id=1, source_target_pairs={{4,5},{6,7},{1,0},{3,2},{12,13},{14,15},{9,8},{11,10},{20,21},{22,... | collective-permute-start | bytes 2371592 | tf_op jit(solution)/shard_map/ppermute | solution.py:301
  42.9 0.0 collective-permute-done.14.refs_14_
  42.9 0.7 %collective-permute-start.6 = (bf16[3104,128]{1,0:T(8,128)(2,1)S(1)}, bf16[3104,128]{1,0:T(8,128)(2,1)S(1)}, u32[]{:S(2)}, u32[]{:S(2)}) collective-permute-start(bf16[3104,128]{1,0:T(8,128)(2,1)S(1)} %collective-permute-done.5.refs_7_), channel_id=1, source_target_pairs={{4,6},{3,1},{12,14},{11,9},{20,22},{19,17},{28,30},{27,25}} | collective-permute-start | bytes 2383880 | tf_op jit(solution)/shard_map/ppermute | solution.py:301
  43.7 0.0 collective-permute-done.10.refs_5_
  43.7 6.1 %collective-permute-done.11.refs_8_ = bf16[3088,128]{1,0:T(8,128)(2,1)S(1)} collective-permute-done((bf16[3088,128]{1,0:T(8,128)(2,1)S(1)}, bf16[3088,128]{1,0:T(8,128)(2,1)S(1)}, u32[]{:S(2)}, u32[]{:S(2)}) %collective-permute-start.11) | collective-permute-done | bytes 790560 | tf_op jit(solution)/shard_map/ppermute | solution.py:301
  49.8 1.4 %collective-permute-done.13.refs_9_ = bf16[3088,128]{1,0:T(8,128)(2,1)S(1)} collective-permute-done((bf16[3088,128]{1,0:T(8,128)(2,1)S(1)}, bf16[3088,128]{1,0:T(8,128)(2,1)S(1)}, u32[]{:S(2)}, u32[]{:S(2)}) %collective-permute-start.13) | collective-permute-done | bytes 790560 | tf_op jit(solution)/shard_map/ppermute | solution.py:301
  51.2 0.0 copy-done
  51.2 8.8 %near.1 = (f32[1536,512]{1,0:T(8,128)S(1)}, bf16[1024,512]{1,0:T(8,128)(2,1)S(1)}) custom-call(s32[32]{0:T(128)} %order_ref.1, bf16[3104,128]{1,0:T(8,128)(2,1)S(1)} %pack.1.refs_0_, bf16[3088,128]{1,0:T(8,128)(2,1)S(1)} %collective-permute-done.7.refs_1_, bf16[3104,128]{1,0:T(8,128)(2,1)S(1)} %collective-permute-done.1.refs_2_, ...), custom_call_target="tpu_custom_call" | custom-call | tf_op jit(solution)/shard_map/near/pallas_call | solution.py:195
  60.0 0.0 collective-permute-done.9.mine
  60.1 0.1 slice.35
  60.1 1.3 %collective-permute-start.16 = (bf16[3088,128]{1,0:T(8,128)(2,1)S(1)}, bf16[3088,128]{1,0:T(8,128)(2,1)S(1)}, u32[]{:S(2)}, u32[]{:S(2)}) collective-permute-start(bf16[3088,128]{1,0:T(8,128)(2,1)S(1)} %slice.35), channel_id=1, source_target_pairs={{6,7},{1,0},{14,15},{9,8},{22,23},{17,16},{30,31},{25,24}} | collective-permute-start | bytes 2371592 | tf_op jit(solution)/shard_map/ppermute | solution.py:301
  61.4 0.0 collective-permute-done.6.mine
  61.4 0.1 slice.34
  61.5 1.3 %collective-permute-start.15 = (bf16[3088,128]{1,0:T(8,128)(2,1)S(1)}, bf16[3088,128]{1,0:T(8,128)(2,1)S(1)}, u32[]{:S(2)}, u32[]{:S(2)}) collective-permute-start(bf16[3088,128]{1,0:T(8,128)(2,1)S(1)} %slice.34), channel_id=1, source_target_pairs={{6,7},{1,0},{14,15},{9,8},{22,23},{17,16},{30,31},{25,24}} | collective-permute-start | bytes 2371592 | tf_op jit(solution)/shard_map/ppermute | solution.py:301
  62.8 1.5 %collective-permute-done.16.other = bf16[3088,128]{1,0:T(8,128)(2,1)S(1)} collective-permute-done((bf16[3088,128]{1,0:T(8,128)(2,1)S(1)}, bf16[3088,128]{1,0:T(8,128)(2,1)S(1)}, u32[]{:S(2)}, u32[]{:S(2)}) %collective-permute-start.16) | collective-permute-done | bytes 790560 | tf_op jit(solution)/shard_map/ppermute | solution.py:301
  64.3 1.7 %far.2.total_in = f32[1536,512]{1,0:T(8,128)S(1)} custom-call(bf16[3104,128]{1,0:T(8,128)(2,1)S(1)} %collective-permute-done.9.mine, bf16[3088,128]{1,0:T(8,128)(2,1)S(1)} %collective-permute-done.16.other, bf16[1024,512]{1,0:T(8,128)(2,1)S(1)} %get-tuple-element.22.far_rows, f32[1536,512]{1,0:T(8,128)S(1)} %get-tuple-element.24.total_in), custom_call_target="tpu_custom_call", output_to_operand_aliasing={{}: (3, {})} | custom-call | flops 805306368 | bytes 8388608 | tf_op jit(solution)/shard_map/far/pallas_call | solution.py:261
  66.0 0.9 %collective-permute-done.15.other = bf16[3088,128]{1,0:T(8,128)(2,1)S(1)} collective-permute-done((bf16[3088,128]{1,0:T(8,128)(2,1)S(1)}, bf16[3088,128]{1,0:T(8,128)(2,1)S(1)}, u32[]{:S(2)}, u32[]{:S(2)}) %collective-permute-start.15) | collective-permute-done | bytes 790560 | tf_op jit(solution)/shard_map/ppermute | solution.py:301
  66.9 2.6 %far.3 = f32[1536,512]{1,0:T(8,128)} custom-call(bf16[3104,128]{1,0:T(8,128)(2,1)S(1)} %collective-permute-done.6.mine, bf16[3088,128]{1,0:T(8,128)(2,1)S(1)} %collective-permute-done.15.other, bf16[1024,512]{1,0:T(8,128)(2,1)S(1)} %get-tuple-element.22.far_rows, f32[1536,512]{1,0:T(8,128)S(1)} %far.2.total_in), custom_call_target="tpu_custom_call" | custom-call | flops 805306368 | bytes 8388608 | tf_op jit(solution)/shard_map/far/pallas_call | solution.py:261
  (2 shorter events, 0.1 us)
Async XLA Ops:
  1.6 16.3 %collective-permute-start.1 = (bf16[3104,128]{1,0:T(8,128)(2,1)S(1)}, bf16[3104,128]{1,0:T(8,128)(2,1)S(1)}, u32[]{:S(2)}, u32[]{:S(2)}) collective-permute-start(bf16[3104,128]{1,0:T(8,128)(2,1)S(1)} %pack.1.refs_0_), channel_id=1, source_target_pairs={{0,2},{2,4},{4,6},{3,1},{5,3},{7,5},{8,10},{10,12},{12,14},{11,9},... | collective-permute-start | bytes 2383880 | tf_op jit(solution)/shard_map/ppermute | solution.py:301
  3.7 25.1 %collective-permute-start.3 = (bf16[1024,512]{1,0:T(8,128)(2,1)}, bf16[1024,512]{1,0:T(8,128)(2,1)S(1)}, u32[]{:S(2)}, u32[]{:S(2)}) collective-permute-start(bf16[1024,512]{1,0:T(8,128)(2,1)} %refs_10_.1), channel_id=1, source_target_pairs={{0,8},{8,0},{16,24},{24,16},{1,9},{9,1},{17,25},{25,17},{2,10},{10... | collective-permute-start | bytes 3145736 | tf_op jit(solution)/shard_map/ppermute | solution.py:301
  4.1 24.8 %collective-permute-start.4 = (bf16[1024,512]{1,0:T(8,128)(2,1)}, bf16[1024,512]{1,0:T(8,128)(2,1)S(1)}, u32[]{:S(2)}, u32[]{:S(2)}) collective-permute-start(bf16[1024,512]{1,0:T(8,128)(2,1)} %refs_10_.1), channel_id=1, source_target_pairs={{0,16},{8,24},{16,0},{24,8},{1,17},{9,25},{17,1},{25,9},{2,18},{10... | collective-permute-start | bytes 3145736 | tf_op jit(solution)/shard_map/ppermute | solution.py:301
  4.3 15.7 %collective-permute-start = (bf16[3104,128]{1,0:T(8,128)(2,1)S(1)}, bf16[3104,128]{1,0:T(8,128)(2,1)S(1)}, u32[]{:S(2)}, u32[]{:S(2)}) collective-permute-start(bf16[3104,128]{1,0:T(8,128)(2,1)S(1)} %pack.1.refs_0_), channel_id=1, source_target_pairs={{1,2},{3,4},{5,6},{2,1},{4,3},{6,5},{9,10},{11,12},{13,14},{10,9},... | collective-permute-start | bytes 2383880 | tf_op jit(solution)/shard_map/ppermute | solution.py:301
  5.1 14.2 %collective-permute-start.7 = (bf16[3088,128]{1,0:T(8,128)(2,1)S(1)}, bf16[3088,128]{1,0:T(8,128)(2,1)S(1)}, u32[]{:S(2)}, u32[]{:S(2)}) collective-permute-start(bf16[3088,128]{1,0:T(8,128)(2,1)S(1)} %slice.37), channel_id=1, source_target_pairs={{0,1},{2,3},{4,5},{6,7},{1,0},{3,2},{5,4},{7,6},{8,9},{10,11},{12,... | collective-permute-start | bytes 2371592 | tf_op jit(solution)/shard_map/ppermute | solution.py:301
  18.0 10.9 %collective-permute-start.2 = (bf16[3088,128]{1,0:T(8,128)(2,1)S(1)}, bf16[3088,128]{1,0:T(8,128)(2,1)S(1)}, u32[]{:S(2)}, u32[]{:S(2)}) collective-permute-start(bf16[3088,128]{1,0:T(8,128)(2,1)S(1)} %slice.36), channel_id=1, source_target_pairs={{2,3},{4,5},{6,7},{1,0},{3,2},{5,4},{10,11},{12,13},{14,15},{9,8},... | collective-permute-start | bytes 2371592 | tf_op jit(solution)/shard_map/ppermute | solution.py:301
  19.3 12.0 %collective-permute-start.8 = (bf16[3104,128]{1,0:T(8,128)(2,1)S(1)}, bf16[3104,128]{1,0:T(8,128)(2,1)S(1)}, u32[]{:S(2)}, u32[]{:S(2)}) collective-permute-start(bf16[3104,128]{1,0:T(8,128)(2,1)S(1)} %collective-permute-done.1.refs_2_), channel_id=1, source_target_pairs={{2,4},{4,6},{3,1},{5,3},{10,12},{12,14},{11,9},{13,11},{18,20},{20... | collective-permute-start | bytes 2383880 | tf_op jit(solution)/shard_map/ppermute | solution.py:301
  28.9 4.5 %collective-permute-start.5 = (bf16[3104,128]{1,0:T(8,128)(2,1)S(1)}, bf16[3104,128]{1,0:T(8,128)(2,1)S(1)}, u32[]{:S(2)}, u32[]{:S(2)}) collective-permute-start(bf16[3104,128]{1,0:T(8,128)(2,1)S(1)} %collective-permute-done.refs_3_), channel_id=1, source_target_pairs={{2,4},{4,6},{3,1},{5,3},{10,12},{12,14},{11,9},{13,11},{18,20},{20... | collective-permute-start | bytes 2383880 | tf_op jit(solution)/shard_map/ppermute | solution.py:301
  29.7 21.5 %copy-start = (bf16[1024,512]{1,0:T(8,128)(2,1)S(1)}, bf16[1024,512]{1,0:T(8,128)(2,1)}, u32[]{:S(2)}) copy-start(bf16[1024,512]{1,0:T(8,128)(2,1)} %refs_10_.1) | copy-start | bytes 3145732
  29.7 12.0 %collective-permute-start.12 = (bf16[512,512]{1,0:T(8,128)(2,1)S(1)}, bf16[512,512]{1,0:T(8,128)(2,1)S(1)}, u32[]{:S(2)}, u32[]{:S(2)}) collective-permute-start(bf16[512,512]{1,0:T(8,128)(2,1)S(1)} %slice.41), channel_id=1, source_target_pairs={{0,16},{8,24},{16,0},{24,8},{1,17},{9,25},{17,1},{25,9},{2,18},{10... | collective-permute-start | bytes 1572872 | tf_op jit(solution)/shard_map/ppermute | solution.py:301
  30.0 12.9 %collective-permute-start.14 = (bf16[512,512]{1,0:T(8,128)(2,1)S(1)}, bf16[512,512]{1,0:T(8,128)(2,1)S(1)}, u32[]{:S(2)}, u32[]{:S(2)}) collective-permute-start(bf16[512,512]{1,0:T(8,128)(2,1)S(1)} %slice.42), channel_id=1, source_target_pairs={{0,8},{8,0},{16,24},{24,16},{1,9},{9,1},{17,25},{25,17},{2,10},{10... | collective-permute-start | bytes 1572872 | tf_op jit(solution)/shard_map/ppermute | solution.py:301
  31.3 28.8 %collective-permute-start.9 = (bf16[3104,128]{1,0:T(8,128)(2,1)S(1)}, bf16[3104,128]{1,0:T(8,128)(2,1)S(1)}, u32[]{:S(2)}, u32[]{:S(2)}) collective-permute-start(bf16[3104,128]{1,0:T(8,128)(2,1)S(1)} %collective-permute-done.8.refs_6_), channel_id=1, source_target_pairs={{4,6},{3,1},{12,14},{11,9},{20,22},{19,17},{28,30},{27,25}} | collective-permute-start | bytes 2383880 | tf_op jit(solution)/shard_map/ppermute | solution.py:301
  32.0 11.6 %collective-permute-start.10 = (bf16[3088,128]{1,0:T(8,128)(2,1)S(1)}, bf16[3088,128]{1,0:T(8,128)(2,1)S(1)}, u32[]{:S(2)}, u32[]{:S(2)}) collective-permute-start(bf16[3088,128]{1,0:T(8,128)(2,1)S(1)} %slice.38), channel_id=1, source_target_pairs={{2,3},{4,5},{6,7},{1,0},{3,2},{5,4},{10,11},{12,13},{14,15},{9,8},... | collective-permute-start | bytes 2371592 | tf_op jit(solution)/shard_map/ppermute | solution.py:301
  33.4 16.4 %collective-permute-start.11 = (bf16[3088,128]{1,0:T(8,128)(2,1)S(1)}, bf16[3088,128]{1,0:T(8,128)(2,1)S(1)}, u32[]{:S(2)}, u32[]{:S(2)}) collective-permute-start(bf16[3088,128]{1,0:T(8,128)(2,1)S(1)} %slice.39), channel_id=1, source_target_pairs={{4,5},{6,7},{1,0},{3,2},{12,13},{14,15},{9,8},{11,10},{20,21},{22,... | collective-permute-start | bytes 2371592 | tf_op jit(solution)/shard_map/ppermute | solution.py:301
  41.6 9.6 %collective-permute-start.13 = (bf16[3088,128]{1,0:T(8,128)(2,1)S(1)}, bf16[3088,128]{1,0:T(8,128)(2,1)S(1)}, u32[]{:S(2)}, u32[]{:S(2)}) collective-permute-start(bf16[3088,128]{1,0:T(8,128)(2,1)S(1)} %slice.40), channel_id=1, source_target_pairs={{4,5},{6,7},{1,0},{3,2},{12,13},{14,15},{9,8},{11,10},{20,21},{22,... | collective-permute-start | bytes 2371592 | tf_op jit(solution)/shard_map/ppermute | solution.py:301
  42.9 18.5 %collective-permute-start.6 = (bf16[3104,128]{1,0:T(8,128)(2,1)S(1)}, bf16[3104,128]{1,0:T(8,128)(2,1)S(1)}, u32[]{:S(2)}, u32[]{:S(2)}) collective-permute-start(bf16[3104,128]{1,0:T(8,128)(2,1)S(1)} %collective-permute-done.5.refs_7_), channel_id=1, source_target_pairs={{4,6},{3,1},{12,14},{11,9},{20,22},{19,17},{28,30},{27,25}} | collective-permute-start | bytes 2383880 | tf_op jit(solution)/shard_map/ppermute | solution.py:301
  60.1 4.2 %collective-permute-start.16 = (bf16[3088,128]{1,0:T(8,128)(2,1)S(1)}, bf16[3088,128]{1,0:T(8,128)(2,1)S(1)}, u32[]{:S(2)}, u32[]{:S(2)}) collective-permute-start(bf16[3088,128]{1,0:T(8,128)(2,1)S(1)} %slice.35), channel_id=1, source_target_pairs={{6,7},{1,0},{14,15},{9,8},{22,23},{17,16},{30,31},{25,24}} | collective-permute-start | bytes 2371592 | tf_op jit(solution)/shard_map/ppermute | solution.py:301
  61.5 5.4 %collective-permute-start.15 = (bf16[3088,128]{1,0:T(8,128)(2,1)S(1)}, bf16[3088,128]{1,0:T(8,128)(2,1)S(1)}, u32[]{:S(2)}, u32[]{:S(2)}) collective-permute-start(bf16[3088,128]{1,0:T(8,128)(2,1)S(1)} %slice.34), channel_id=1, source_target_pairs={{6,7},{1,0},{14,15},{9,8},{22,23},{17,16},{30,31},{25,24}} | collective-permute-start | bytes 2371592 | tf_op jit(solution)/shard_map/ppermute | solution.py:301
